TPU v7x, 768 devices: a whole 4x8x12 slice. The times are simulated.
768 devices in a mesh: pipe: 24 (over z_lo, y), dp: 32 (over z_hi, x, core).
Axes of the slice: x: 4, y: 8, z: 12 (z_hi: 4, z_lo: 3; z = z_hi * 3 + z_lo), core: 2. Of those that a mesh axis runs over, the one named last changes fastest.
Arguments:
- hidden: bfloat16 [192, 7168], P('dp'), may hold values from -48 to 48
- head_weight: bfloat16 [98304, 7168], P(('pipe', 'dp')), may hold values from -48 to 48
- token_ids: int32 [192], replicated, may hold values from 0 to 98303
- segment_ids: int32 [192], replicated, may hold values from 0 to 15, never falling along the last dimension, each value on 1 to 16 neighbouring positions
Outputs:
- row_grad: bfloat16 [192, 7168], P('dp')
- weight_grad: bfloat16 [98304, 7168], P(('pipe', 'dp'))
- target_rows: bfloat16 [192, 7168], P('dp')
- mean_loss: float32 [], replicated
All inputs are finite; a program needn't handle non-finite values.
Results may differ from a plain program's by a relative error of at most 0.0049.
Values may be sent and summed in bfloat16 or wider, within the bound.
A program may use at most 64 MiB of HBM per device.

v0:
```python
import jax
import jax.numpy as jnp
from jax import lax
from jax.sharding import PartitionSpec as P

SEG_MEAN = 12


LOSS_SCALE = 4096.0


def token_weights(token_ids, segment_ids, turn_count):
    ahead_ids = jnp.concatenate([token_ids[2:], jnp.zeros((2,), jnp.int32)])
    ahead_segment = jnp.concatenate([segment_ids[2:], jnp.full((2,), -1, jnp.int32)])
    is_valid = (ahead_segment == segment_ids).astype(jnp.float32)
    member = (segment_ids[:, None] == jnp.arange(turn_count, dtype=jnp.int32)[None, :]).astype(
        jnp.float32
    )
    counts = jnp.sum(member * is_valid[:, None], axis=0)
    per_token = jnp.sum(member * counts[None, :], axis=1)
    weight = is_valid / (jnp.maximum(per_token, 1.0) * turn_count)
    return (ahead_ids, weight)


def body(hidden, head_weight, token_ids, segment_ids):
    row_count = token_ids.shape[0]
    ahead_ids, weight = token_weights(token_ids, segment_ids, row_count // SEG_MEAN)
    tok_rows, model_width = hidden.shape
    vocab_rows = head_weight.shape[0]
    pipe_count = lax.axis_size("pipe")
    data_count = lax.axis_size("dp")
    piece_length = tok_rows * model_width // pipe_count
    own_weight = lax.dynamic_slice_in_dim(weight, lax.axis_index("dp") * tok_rows, tok_rows, 0)
    target_rows = (-LOSS_SCALE * own_weight[:, None] * hidden.astype(jnp.float32)).astype(
        jnp.bfloat16
    )
    gathered = lax.all_gather(hidden, "dp", axis=0, tiled=True)
    logits = lax.dot_general(
        gathered, head_weight, (((1,), (1,)), ((), ())), preferred_element_type=jnp.float32
    )
    offset = (lax.axis_index("pipe") * data_count + lax.axis_index("dp")) * vocab_rows
    target_hit = ahead_ids[:, None] - offset == jnp.arange(vocab_rows, dtype=jnp.int32)[None, :]
    local_peak = jnp.max(logits, axis=1)
    row_peak = lax.pmax(local_peak, ("pipe", "dp"))
    spread = jnp.sum(jnp.exp(logits - row_peak[:, None]), axis=1)
    picked = jnp.sum(jnp.where(target_hit, logits, 0.0), axis=1)
    spread, picked = lax.psum((spread, picked), ("pipe", "dp"))
    log_total = row_peak + jnp.log(spread)
    mean_loss = jnp.sum(weight * (log_total - picked))
    scaled = LOSS_SCALE * weight[:, None]
    probs = jnp.exp(logits - log_total[:, None])
    logit_grads = (scaled * (probs - target_hit.astype(jnp.float32))).astype(jnp.bfloat16)
    prob_grads = (scaled * probs).astype(jnp.bfloat16)
    weight_grad = lax.dot_general(
        prob_grads, gathered, (((0,), (0,)), ((), ())), preferred_element_type=jnp.float32
    ).astype(jnp.bfloat16)
    own_rows = lax.psum_scatter(
        jnp.dot(logit_grads, head_weight, preferred_element_type=jnp.float32),
        "dp",
        scatter_dimension=0,
        tiled=True,
    )
    arranged = own_rows.reshape(pipe_count, piece_length)
    own_piece = lax.psum_scatter(arranged, "pipe", scatter_dimension=0, tiled=True)
    pieces = lax.all_gather(own_piece.astype(jnp.bfloat16), "pipe", axis=0, tiled=True)
    row_grad = pieces.reshape(tok_rows, model_width)
    return (row_grad, weight_grad, target_rows, mean_loss)


def solution(mesh):
    placed = (P("dp", None), P(("pipe", "dp"), None), P(), P())
    return jax.shard_map(
        body,
        mesh=mesh,
        in_specs=placed,
        out_specs=(P("dp", None), P(("pipe", "dp"), None), P("dp", None), P()),
        check_vma=False,
    )
```

profile of v0, /device:TPU:392, one launch (start us, length us, event | category | flops | bytes accessed | tf_op | source)
XLA Modules:
  0.0 787.4 jit_solution(6030564781342244890)
XLA Ops:
  7.2 0.0 copy-start
  7.2 0.0 all-gather.4.cloned.1.call-start
  7.2 0.7 all-gather.4.cloned.1.call-update
  7.9 1.3 dynamic-slice.6
  9.2 0.7 slice.7
  10.0 0.7 slice.6
  10.7 1.3 dynamic-slice.2
  12.6 0.7 compare_convert_fusion
  13.3 0.8 select_reduce_fusion.2
  14.1 0.8 select_reduce_fusion.1
  14.9 76.6 %all-gather.4.cloned.1.call-done = bf16[32,6,7168]{2,1,0:T(8,128)(2,1)} async-done(((bf16[1,6,7168]{2,1,0:T(8,128)(2,1)}), bf16[32,6,7168]{2,1,0:T(8,128)(2,1)}) %all-gather.4.cloned.1.call-update) | async-done | bytes 2752528 | tf_op jit(solution)/shard_map/all_gather | solution.py:37
  91.5 4.7 reshape.28
  96.2 0.0 copy-done
  96.2 2.7 fusion.8
  98.9 105.3 %pmax.7 = f32[192]{0:T(256)S(1)} all-reduce(f32[192]{0:T(256)S(1)} %get-tuple-element.11), channel_id=1, replica_groups=mesh['pipe'=24,'dp'=32] {'pipe','dp'}, use_global_device_ids=true, to_apply=%region_3.0 | all-reduce | flops 192 | bytes 1536 | tf_op jit(solution)/shard_map/pmax | solution.py:44
  204.2 0.2 select_reduce_fusion
  204.4 104.2 %all-reduce.5 = (f32[192]{0:T(256)S(1)}, f32[192]{0:T(256)S(1)}) all-reduce(f32[192]{0:T(256)S(1)} %get-tuple-element.5, f32[192]{0:T(256)S(1)} %get-tuple-element.4), channel_id=1, replica_groups=mesh['pipe'=24,'dp'=32] {'pipe','dp'}, use_global_device_ids=true, to_apply=%region_5.6 | all-reduce | flops 384 | bytes 3072 | tf_op jit(solution)/shard_map/psum | solution.py:47
  308.6 0.6 multiply_reduce_fusion
  309.2 3.3 fusion.1
  312.5 0.0 copy-start.1
  312.6 146.4 %fusion = f32[8,7168]{1,0:T(8,128)S(1)} fusion(f32[192,7168]{1,0:T(8,128)} %fusion.1), kind=kCustom, calls=%all-reduce-scatter | all-reduce-scatter fusion | flops 1835009 | bytes 5738496
  459.0 1.9 collective-permute-start.6
  460.9 1.9 collective-permute-start.5
  462.8 1.9 collective-permute-start.4
  464.8 4.5 collective-permute-start.3
  469.3 0.1 dynamic-slice_multiply_fusion
  469.4 3.8 collective-permute-start.7
  473.2 0.0 copy-done.1
  473.2 0.7 multiply_convert_fusion
  473.9 13.5 %collective-permute-done.7 = f32[6,7168]{1,0:T(8,128)S(1)} collective-permute-done((f32[6,7168]{1,0:T(8,128)S(1)}, f32[6,7168]{1,0:T(8,128)S(1)}, u32[]{:S(2)}, u32[]{:S(2)}) %collective-permute-start.7) | collective-permute-done | bytes 172064
  487.4 1.9 collective-permute-start.2
  489.3 0.0 collective-permute-done.6
  489.4 14.6 %collective-permute-start.1 = (f32[8,7168]{1,0:T(8,128)S(1)}, f32[8,7168]{1,0:T(8,128)S(1)}, u32[]{:S(2)}, u32[]{:S(2)}) collective-permute-start(f32[8,7168]{1,0:T(8,128)S(1)} %fusion), channel_id=1, source_target_pairs={{0,2},{1,3},{2,4},{3,5},{4,6},{5,7},{6,8},{7,9},{8,10},{9,11},{10,... | collective-permute-start | bytes 688136
  504.0 0.0 collective-permute-done.5
  504.0 2.8 collective-permute-start
  506.8 3.8 convolution_convert_fusion
  510.6 0.0 collective-permute-done.4
  510.6 0.0 collective-permute-done.3
  510.6 0.5 collective-permute-done.2
  511.1 0.0 copy-start.2
  511.1 0.0 collective-permute-done.1
  511.2 0.7 copy-done.2
  511.8 0.0 copy-start.3
  511.8 0.7 copy-done.3
  512.5 45.2 %collective-permute-done = f32[8,7168]{1,0:T(8,128)} collective-permute-done((f32[8,7168]{1,0:T(8,128)S(1)}, f32[8,7168]{1,0:T(8,128)}, u32[]{:S(2)}, u32[]{:S(2)}) %collective-permute-start) | collective-permute-done | bytes 229408
  557.8 26.3 %concatenate.8 = f32[70,7168]{1,0:T(8,128)} concatenate(f32[6,7168]{1,0:T(8,128)S(1)} %collective-permute-done.7, f32[8,7168]{1,0:T(8,128)S(1)} %collective-permute-done.6, f32[8,7168]{1,0:T(8,128)S(1)} %collective-permute-done.5, f32[8,7168]{1,0:T(8,128)S(1)} %collective-permute-done.4, f32[8,7168]{1,0:T(8,128)S(1)} %collective-permute-done.3, f32[8,7168]{1,0:T(8,128)} %copy-done.2, ...), dimensions={0} | concatenate | bytes 4014080
  584.1 1.0 constant_dynamic-slice_fusion
  585.1 0.1 reshape.25
  585.2 129.5 %all-reduce.7 = bf16[24,1792]{1,0:T(8,128)(2,1)S(1)} all-reduce(f32[24,1792]{1,0:T(8,128)S(1)} %reshape.25), channel_id=3, replica_groups=mesh['pipe'=24,'dp'=32] {'pipe'}, use_global_device_ids=true, to_apply=%region_7.8.clone | all-reduce | flops 43008 | bytes 258048
  714.7 0.7 fusion.7
  715.4 64.0 %all-gather.1 = bf16[24,1,1792]{2,1,0:T(2,128)(2,1)S(1)} all-gather(bf16[1,1,1792]{2,1,0:T(2,128)(2,1)S(1)} %fusion.7), channel_id=1, replica_groups=mesh['pipe'=24,'dp'=32] {'pipe'}, dimensions={0}, use_global_device_ids=true | all-gather | bytes 89600 | tf_op jit(solution)/shard_map/all_gather | solution.py:65
  779.4 0.5 reduce
  779.9 0.7 reshape.26
  (3 shorter events, 0.0 us)
Async XLA Ops:
  7.2 89.0 %copy-start = (bf16[128,7168]{1,0:T(8,128)(2,1)S(1)}, bf16[128,7168]{1,0:T(8,128)(2,1)}, u32[]{:S(2)}) copy-start(bf16[128,7168]{1,0:T(8,128)(2,1)} %param.5) | copy-start | bytes 5505028
  7.2 84.3 %all-gather.4.cloned.1.call-start = ((), (), s32[]{:S(2)}) async-start(), calls=%async_computation | async-start | bytes 3784704 | tf_op jit(solution)/shard_map/all_gather | solution.py:37
  312.5 160.6 %copy-start.1 = (bf16[6,7168]{1,0:T(8,128)(2,1)S(1)}, bf16[6,7168]{1,0:T(8,128)(2,1)}, u32[]{:S(2)}) copy-start(bf16[6,7168]{1,0:T(8,128)(2,1)} %param.4) | copy-start | bytes 258052
  459.0 30.4 %collective-permute-start.6 = (f32[8,7168]{1,0:T(8,128)S(1)}, f32[8,7168]{1,0:T(8,128)S(1)}, u32[]{:S(2)}, u32[]{:S(2)}) collective-permute-start(f32[8,7168]{1,0:T(8,128)S(1)} %fusion), channel_id=1, source_target_pairs={{0,7},{1,8},{2,9},{3,10},{4,11},{5,12},{6,13},{7,14},{8,15},{9,16}... | collective-permute-start | bytes 688136
  460.9 43.1 %collective-permute-start.5 = (f32[8,7168]{1,0:T(8,128)S(1)}, f32[8,7168]{1,0:T(8,128)S(1)}, u32[]{:S(2)}, u32[]{:S(2)}) collective-permute-start(f32[8,7168]{1,0:T(8,128)S(1)} %fusion), channel_id=1, source_target_pairs={{0,6},{1,7},{2,8},{3,9},{4,10},{5,11},{6,12},{7,13},{8,14},{9,15},... | collective-permute-start | bytes 688136
  462.8 47.8 %collective-permute-start.4 = (f32[8,7168]{1,0:T(8,128)S(1)}, f32[8,7168]{1,0:T(8,128)S(1)}, u32[]{:S(2)}, u32[]{:S(2)}) collective-permute-start(f32[8,7168]{1,0:T(8,128)S(1)} %fusion), channel_id=1, source_target_pairs={{0,5},{1,6},{2,7},{3,8},{4,9},{5,10},{6,11},{7,12},{8,13},{9,14},{... | collective-permute-start | bytes 688136
  464.8 45.8 %collective-permute-start.3 = (f32[8,7168]{1,0:T(8,128)S(1)}, f32[8,7168]{1,0:T(8,128)S(1)}, u32[]{:S(2)}, u32[]{:S(2)}) collective-permute-start(f32[8,7168]{1,0:T(8,128)S(1)} %fusion), channel_id=1, source_target_pairs={{0,4},{1,5},{2,6},{3,7},{4,8},{5,9},{6,10},{7,11},{8,12},{9,13},{1... | collective-permute-start | bytes 688136
  469.4 18.0 %collective-permute-start.7 = (f32[6,7168]{1,0:T(8,128)S(1)}, f32[6,7168]{1,0:T(8,128)S(1)}, u32[]{:S(2)}, u32[]{:S(2)}) collective-permute-start(f32[6,7168]{1,0:T(8,128)S(1)} %slice.8), channel_id=1, source_target_pairs={{0,8},{1,9},{2,10},{3,11},{4,12},{5,13},{6,14},{7,15},{8,16},{9,17... | collective-permute-start | bytes 516104
  487.4 23.7 %collective-permute-start.2 = (f32[8,7168]{1,0:T(8,128)S(1)}, f32[8,7168]{1,0:T(8,128)S(1)}, u32[]{:S(2)}, u32[]{:S(2)}) collective-permute-start(f32[8,7168]{1,0:T(8,128)S(1)} %fusion), channel_id=1, source_target_pairs={{0,3},{1,4},{2,5},{3,6},{4,7},{5,8},{6,9},{7,10},{8,11},{9,12},{10... | collective-permute-start | bytes 688136
  489.4 21.8 %collective-permute-start.1 = (f32[8,7168]{1,0:T(8,128)S(1)}, f32[8,7168]{1,0:T(8,128)S(1)}, u32[]{:S(2)}, u32[]{:S(2)}) collective-permute-start(f32[8,7168]{1,0:T(8,128)S(1)} %fusion), channel_id=1, source_target_pairs={{0,2},{1,3},{2,4},{3,5},{4,6},{5,7},{6,8},{7,9},{8,10},{9,11},{10,... | collective-permute-start | bytes 688136
  504.0 53.8 %collective-permute-start = (f32[8,7168]{1,0:T(8,128)S(1)}, f32[8,7168]{1,0:T(8,128)}, u32[]{:S(2)}, u32[]{:S(2)}) collective-permute-start(f32[8,7168]{1,0:T(8,128)S(1)} %fusion), channel_id=1, source_target_pairs={{0,1},{1,2},{2,3},{3,4},{4,5},{5,6},{6,7},{7,8},{8,9},{9,10},{10,1... | collective-permute-start | bytes 688136
  511.1 0.7 copy-start.2
  511.8 0.7 copy-start.3
Sparse Core Ops, SparseCore 0:
  11.7 79.7 all-gather.3
where the time goes:
time: 789 us; the launch traced here: 787 us
  blocking collectives  549 us (70%)
  waiting for transfers between devices  137 us (17%)
  local copies, waits for them, and re-layouts  38.9 us (5%)
  starting transfers between devices  33.5 us (4%)
  between operations  14.9 us (2%)
  matrix products  9.85 us (1%)
    unnamed x2, blocking collectives  276 us
    pmax x1, blocking collectives, body(): row_peak = lax.pmax(local_peak, ('pipe', 'dp'))  105 us
    psum x1, blocking collectives, body(): spread, picked = lax.psum((spread, picked), ('pipe', 'dp'))  104 us
    all_gather x1, waiting for transfers between devices, body(): gathered = lax.all_gather(hidden, 'dp', axis=0, tiled=True)  76.6 us
    all_gather x1, blocking collectives, body(): lax.all_gather(own_piece.astype(jnp.bfloat16), 'pipe', axis=0, tiled=True)  64 us
    unnamed x9, waiting for transfers between devices  60 us
    unnamed x15, local copies, waits for them, and re-layouts  36.7 us
    unnamed x8, starting transfers between devices  33.4 us
  transfers between devices with their start and end apart: 9, of which 4 were waited for; matrix products, arithmetic and copies ran while one was open for 1% of the time, Pallas kernels for 0%

commit v1 on v0

v1 whole, which is shorter than its diff:
```python
import functools

import jax
import jax.numpy as jnp
import numpy as np
from jax import lax
from jax.experimental import pallas as pl
from jax.experimental.pallas import tpu as pltpu
from jax.sharding import PartitionSpec as P

MESH = pl.DeviceIdType.MESH
LOSS_SCALE = 4096.0
TURNS = 16
TOKENS = 192
WIDTH = 7168
PIECE = 896
VROWS = 128
BF16 = jnp.bfloat16
F32 = jnp.float32


def permutation():
    perm = np.zeros((TOKENS, TOKENS), np.float32)
    for j in range(8):
        for h in range(4):
            for r in range(6):
                perm[j * 24 + h * 6 + r, h * 48 + j * 6 + r] = 1.0
    return perm


def kernel(
    hid, w_ref, ids, perm_ref,
    rowg, wgrad, trow, loss,
    s1buf, scr48, hp, wg, acc, e_own, st, stx, sty, stz, eb, lgb, pf, pb, r1, r2s, r2, gs, gb, rowf, wgs,
    s1s, s1r, ws, wr, zs, zr, ys, yr, cs, cr, xs, xr, es, er, tys, tyr, tzs, tzr,
    r1ss, r1rs, r2ss, r2rs, gss, grs, outsem,
):
    pipe, dp = lax.axis_index("pipe"), lax.axis_index("dp")
    lo, y = pipe // 8, lax.rem(pipe, 8)
    h, j = dp // 8, lax.rem(dp, 8)
    x, c = j // 2, lax.rem(j, 2)
    z = h * 3 + lo
    cstar = h // 2

    def dev(jj, yy, zz):
        return (lax.rem(zz, 3) * 8 + yy, (zz // 3) * 8 + jj)

    sends = []

    def send(src, dst, ss, rs, to, cond=None):
        d = pltpu.make_async_remote_copy(
            src_ref=src, dst_ref=dst, send_sem=ss, recv_sem=rs, device_id=to, device_id_type=MESH
        )
        if cond is None:
            d.start()
        else:
            pl.when(cond)(d.start)
        sends.append((d, cond))

    def recv(dst, ss, rs, cond=None):
        d = pltpu.make_async_remote_copy(
            src_ref=dst, dst_ref=dst, send_sem=ss, recv_sem=rs,
            device_id=dev(j, lax.rem(y + 1, 8), z), device_id_type=MESH,
        )
        if cond is None:
            d.wait_recv()
        else:
            pl.when(cond)(d.wait_recv)

    bar = pltpu.get_barrier_semaphore()

    def hello(to):
        pl.semaphore_signal(bar, inc=1, device_id=to, device_id_type=MESH)

    for dj in range(1, 8):
        hello(dev(lax.rem(j + dj, 8), y, z))
    for dy in range(1, 8):
        hello(dev(j, lax.rem(y + dy, 8), z))
    for dz in range(1, 12):
        hello(dev(j, y, lax.rem(z + dz, 12)))
    for l3 in range(3):
        for jj in range(8):
            to = dev(jj, j, h * 3 + l3)
            if_other = jnp.logical_or(jnp.logical_or(j != y, jj != j), lo != l3)
            pl.when(if_other)(functools.partial(hello, to))
    pl.semaphore_wait(bar, 25 + 24 - (j == y).astype(jnp.int32))

    col = pl.ds(pl.multiple_of(y * PIECE, 128), PIECE)
    for dx in range(4):
        tx = lax.rem(x + dx, 4)
        send(
            hid.at[:, col], s1buf.at[j], s1s.at[dx], s1r.at[j], dev(tx * 2 + cstar, y, z),
            (c != cstar) if dx == 0 else None,
        )
    for dj in range(1, 8):
        tj = lax.rem(j + dj, 8)
        send(
            w_ref.at[:, pl.ds(pl.multiple_of(tj * PIECE, 128), PIECE)], wg.at[j],
            ws.at[dj], wr.at[j], dev(tj, y, z),
        )
    wg[j] = w_ref[:, pl.ds(pl.multiple_of(j * PIECE, 128), PIECE)]

    tok_ahead = ids[0:1, :]
    seg = ids[1:2, :]
    seg_ahead = ids[2:3, :]
    valid = (seg_ahead == seg).astype(F32)
    member = (lax.broadcasted_iota(jnp.int32, (TURNS, TOKENS), 0) == seg).astype(F32)
    counts = jnp.sum(member * valid, axis=1, keepdims=True)
    per_token = jnp.sum(member * counts, axis=0, keepdims=True)
    weight = valid / (jnp.maximum(per_token, 1.0) * TURNS)
    scaled = LOSS_SCALE * weight
    pick6 = (
        lax.broadcasted_iota(jnp.int32, (6, TOKENS), 1)
        == lax.broadcasted_iota(jnp.int32, (6, TOKENS), 0) + dp * 6
    )
    own_scaled = jnp.sum(jnp.where(pick6, scaled, 0.0), axis=1, keepdims=True)
    trow[...] = (-own_scaled * hid[...].astype(F32)).astype(BF16)

    @pl.when(c == cstar)
    def _():
        s1buf[j] = hid[:, col]
        for jj in range(8):
            recv(s1buf.at[jj], s1s.at[0], s1r.at[jj], jj != j)
        for jj in range(8):
            scr48[6 * jj:6 * jj + 6, :] = s1buf[jj].astype(F32)
        hp[y, h] = scr48[...].astype(BF16)

    for k in range(1, 4):
        send(hp.at[y, h], hp.at[y, h], zs.at[k], zr.at[k], dev(j, y, lax.rem(z + 3 * k, 12)), c == cstar)

    up, down = dev(j, lax.rem(y + 1, 8), z), dev(j, lax.rem(y + 7, 8), z)
    sib = dev(x * 2 + 1 - c, y, z)

    def ring_valid(k, way, s):
        return k <= 3 or (k == 4 and way == s)

    def slot(k, way):
        return 0 if k == 0 else (7 if k == 4 else 1 + 2 * (k - 1) + way)

    def piece(k, way):
        return y if k == 0 else lax.rem(y + (8 - k if way == 0 else k), 8)

    def pass_on(k, way, s):
        blk = hp.at[piece(k, way), 2 * c + s]
        for w in (0, 1):
            if (k == 0 or w == way) and ring_valid(k + 1, w, s):
                send(blk, blk, ys.at[w, s, k], yr.at[w, s, k], up if w == 0 else down)
        send(blk, blk, cs.at[slot(k, way), s], cr.at[slot(k, way), s], sib)

    def logits_of(k, way):
        p = piece(k, way)
        for s in range(2):
            blk = hp.at[p, 2 * (1 - c) + s]
            recv(blk, cs.at[slot(k, way), s], cr.at[slot(k, way), s])
        tile = w_ref[:, pl.ds(pl.multiple_of(p * PIECE, 128), PIECE)]
        tokens = hp[p].reshape(TOKENS, PIECE)
        part = lax.dot_general(tile, tokens, (((1,), (1,)), ((), ())), preferred_element_type=F32)
        if k == 0:
            acc[...] = part
        else:
            acc[...] += part

    for s in range(2):
        for k in range(1, 4):
            src_h = lax.rem(h + 4 - k, 4)
            recv(hp.at[y, src_h], zs.at[k], zr.at[k], src_h == 2 * c + s)
        pass_on(0, 0, s)
    for k in range(1, 5):
        for s in range(2):
            for way in range(2):
                if ring_valid(k, way, s):
                    blk = hp.at[piece(k, way), 2 * c + s]
                    recv(blk, ys.at[way, s, k - 1], yr.at[way, s, k - 1])
                    pass_on(k, way, s)
        logits_of(k - 1, 0)
        if k > 1:
            logits_of(k - 1, 1)
    logits_of(4, 0)

    logits = acc[...]
    vocab0 = (pipe * 32 + dp) * VROWS
    hit = lax.broadcasted_iota(jnp.int32, (VROWS, TOKENS), 0) == tok_ahead - vocab0
    peak = jnp.max(logits, axis=0, keepdims=True)
    ex = jnp.exp(logits - peak)
    total = jnp.sum(ex, axis=0, keepdims=True)
    picked = jnp.sum(jnp.where(hit, logits, 0.0), axis=0, keepdims=True)
    e_own[...] = ex

    def merge(buf, n):
        m = buf[0, 0:1, :]
        for i in range(1, n):
            m = jnp.maximum(m, buf[i, 0:1, :])
        s, p = jnp.zeros_like(m), jnp.zeros_like(m)
        for i in range(n):
            s += buf[i, 1:2, :] * jnp.exp(buf[i, 0:1, :] - m)
            p += buf[i, 2:3, :]
        return m, s, p

    def put(buf, idx, m, s, p):
        buf[idx, 0:1, :] = m
        buf[idx, 1:2, :] = s
        buf[idx, 2:3, :] = p
        buf[idx, 3:8, :] = jnp.zeros((5, TOKENS), F32)

    put(stx, j, peak, total, picked)
    for dj in range(1, 8):
        send(stx.at[j], stx.at[j], xs.at[dj], xr.at[j], dev(lax.rem(j + dj, 8), y, z))
    eb[j] = lax.dot_general(
        perm_ref[...].astype(BF16), ex.astype(BF16), (((1,), (1,)), ((), ())), preferred_element_type=F32
    ).astype(BF16)
    for dj in range(1, 8):
        send(eb.at[j], eb.at[j], es.at[dj], er.at[j], dev(lax.rem(j + dj, 8), y, z))

    for jj in range(8):
        recv(stx.at[jj], xs.at[0], xr.at[jj], jj != j)
    put(sty, y, *merge(stx, 8))
    for dy in range(1, 8):
        send(sty.at[y], sty.at[y], tys.at[dy], tyr.at[y], dev(j, lax.rem(y + dy, 8), z))
    for yy in range(8):
        recv(sty.at[yy], tys.at[0], tyr.at[yy], yy != y)
    put(stz, z, *merge(sty, 8))
    for dz in range(1, 12):
        send(stz.at[z], stz.at[z], tzs.at[dz], tzr.at[z], dev(j, y, lax.rem(z + dz, 12)))
    for zz in range(12):
        recv(stz.at[zz], tzs.at[0], tzr.at[zz], zz != z)
    m_all, s_all, p_all = merge(stz, 12)
    log_total = m_all + jnp.log(s_all)
    loss[...] = jnp.sum(weight * (log_total - p_all), axis=1, keepdims=True)

    for jj in range(8):
        st[jj:jj + 1, :] = scaled * jnp.exp(stx[jj, 0:1, :] - log_total)
    st[8:9, :] = scaled
    st[9:10, :] = tok_ahead.astype(F32)
    st[10:16, :] = jnp.zeros((6, TOKENS), F32)
    cols = lax.dot_general(
        perm_ref[...], st[...], (((1,), (1,)), ((), ())),
        preferred_element_type=F32, precision=lax.Precision.HIGHEST,
    )
    lane = lax.broadcasted_iota(jnp.int32, (TOKENS, VROWS), 1)
    ahead_col = jnp.round(cols[:, 9:10]).astype(jnp.int32)
    for jj in range(8):
        recv(eb.at[jj], es.at[0], er.at[jj], jj != j)
        vocab_j = (pipe * 32 + h * 8 + jj) * VROWS
        hit_j = lane == ahead_col - vocab_j
        lg = cols[:, jj:jj + 1] * eb[jj].astype(F32) - jnp.where(hit_j, cols[:, 8:9], 0.0)
        lgb[:, jj * VROWS:(jj + 1) * VROWS] = lg.astype(BF16)
    for jj in range(8):
        recv(wg.at[jj], ws.at[0], wr.at[jj], jj != j)
    part = jnp.dot(lgb[...], wg[...].reshape(8 * VROWS, PIECE), preferred_element_type=F32)
    pf[...] = part.reshape(8, 24, PIECE)
    pb[...] = pf[...].astype(BF16)

    for dy in range(1, 8):
        ty = lax.rem(y + dy, 8)
        send(pb.at[ty], r1.at[y], r1ss.at[dy], r1rs.at[y], dev(j, ty, z))

    probs = (scaled * (e_own[...] * jnp.exp(peak - log_total))).astype(BF16)
    for p in range(8):
        wgs[:, p * PIECE:(p + 1) * PIECE] = jnp.dot(
            probs, hp[p].reshape(TOKENS, PIECE), preferred_element_type=F32
        ).astype(BF16)
    out = pltpu.make_async_copy(wgs, wgrad, outsem)
    out.start()

    r1[y] = jnp.zeros((24, PIECE), BF16)
    tot = pf[y]
    for yy in range(8):
        recv(r1.at[yy], r1ss.at[0], r1rs.at[yy], yy != y)
        tot += r1[yy].astype(F32)
    for zz in range(12):
        r2s[zz] = tot[2 * zz:2 * zz + 2, :]
    for dz in range(1, 12):
        tz = lax.rem(z + dz, 12)
        send(r2s.at[tz], r2.at[z], r2ss.at[dz], r2rs.at[z], dev(j, y, tz))
    r2[z] = r2s[z]
    fin = jnp.zeros((2, PIECE), F32)
    for zz in range(12):
        recv(r2.at[zz], r2ss.at[0], r2rs.at[zz], zz != z)
        fin += r2[zz]
    gs[...] = fin.astype(BF16)

    for l3 in range(3):
        for yy in range(8):
            to = dev(y, yy, h * 3 + l3)
            other = jnp.logical_or(jnp.logical_or(j != y, yy != y), lo != l3)
            send(gs, gb.at[lo, j], gss.at[l3, yy], grs.at[lo, j], to, other)

    @pl.when(j == y)
    def _():
        gb[lo, j] = gs[...]

    for l3 in range(3):
        for jj in range(8):
            other = jnp.logical_or(jnp.logical_or(j != y, jj != j), lo != l3)
            recv(gb.at[l3, jj], gss.at[0, 0], grs.at[l3, jj], other)
            rowf[2 * l3:2 * l3 + 2, jj * PIECE:(jj + 1) * PIECE] = gb[l3, jj].astype(F32)
    rowg[...] = rowf[0:6, :].astype(BF16)

    for d, cond in sends:
        if cond is None:
            d.wait_send()
        else:
            pl.when(cond)(d.wait_send)
    out.wait()


def body(hidden, head_weight, token_ids, segment_ids):
    zeros = jnp.zeros((2,), jnp.int32)
    ids = jnp.stack(
        [
            jnp.concatenate([token_ids[2:], zeros]),
            segment_ids,
            jnp.concatenate([segment_ids[2:], zeros - 1]),
        ]
        + [segment_ids] * 5
    )
    dma = pltpu.SemaphoreType.DMA
    vmem = pl.BlockSpec(memory_space=pltpu.VMEM)
    row_grad, weight_grad, target_rows, loss = pl.pallas_call(
        kernel,
        out_shape=(
            jax.ShapeDtypeStruct((6, WIDTH), BF16),
            jax.ShapeDtypeStruct((VROWS, WIDTH), BF16),
            jax.ShapeDtypeStruct((6, WIDTH), BF16),
            jax.ShapeDtypeStruct((1, 1), F32),
        ),
        in_specs=[vmem] * 4,
        out_specs=(vmem, pl.BlockSpec(memory_space=pl.ANY), vmem, vmem),
        scratch_shapes=[
            pltpu.VMEM((8, 6, PIECE), BF16),
            pltpu.VMEM((48, PIECE), F32),
            pltpu.VMEM((8, 4, 48, PIECE), BF16),
            pltpu.VMEM((8, VROWS, PIECE), BF16),
            pltpu.VMEM((VROWS, TOKENS), F32),
            pltpu.VMEM((VROWS, TOKENS), F32),
            pltpu.VMEM((16, TOKENS), F32),
            pltpu.VMEM((8, 8, TOKENS), F32),
            pltpu.VMEM((8, 8, TOKENS), F32),
            pltpu.VMEM((12, 8, TOKENS), F32),
            pltpu.VMEM((8, TOKENS, VROWS), BF16),
            pltpu.VMEM((TOKENS, 8 * VROWS), BF16),
            pltpu.VMEM((8, 24, PIECE), F32),
            pltpu.VMEM((8, 24, PIECE), BF16),
            pltpu.VMEM((8, 24, PIECE), BF16),
            pltpu.VMEM((12, 2, PIECE), F32),
            pltpu.VMEM((12, 2, PIECE), F32),
            pltpu.VMEM((2, PIECE), BF16),
            pltpu.VMEM((3, 8, 2, PIECE), BF16),
            pltpu.VMEM((8, WIDTH), F32),
            pltpu.VMEM((VROWS, WIDTH), BF16),
            dma((4,)), dma((8,)), dma((8,)), dma((8,)), dma((4,)), dma((4,)),
            dma((2, 2, 4)), dma((2, 2, 4)), dma((8, 2)), dma((8, 2)),
            dma((8,)), dma((8,)), dma((8,)), dma((8,)), dma((8,)), dma((8,)), dma((12,)), dma((12,)),
            dma((8,)), dma((8,)), dma((12,)), dma((12,)), dma((3, 8)), dma((3, 8)), dma,
        ],
        compiler_params=pltpu.CompilerParams(
            collective_id=0, has_side_effects=True, vmem_limit_bytes=40 * 2**20
        ),
    )(hidden, head_weight, ids, jnp.asarray(permutation()))
    return (row_grad, weight_grad, target_rows, loss.reshape(()))


def solution(mesh):
    placed = (P("dp", None), P(("pipe", "dp"), None), P(), P())
    return jax.shard_map(
        body,
        mesh=mesh,
        in_specs=placed,
        out_specs=(P("dp", None), P(("pipe", "dp"), None), P("dp", None), P()),
        check_vma=False,
    )
```

time: 789 us -> 112 us (0.14)
  the two profiles are of different devices: /device:TPU:392 before, /device:TPU:6 now
where the time goes in v1:
time: 112 us; the launch traced here: 111 us
  Pallas kernels  101 us (90%)
  local copies, waits for them, and re-layouts  8.27 us (7%)
  between operations  2.39 us (2%)
    pallas_call x1, Pallas kernels, body(): pl.pallas_call(kernel, out_shape=(jax.ShapeDtypeStruct((6, WIDTH), BF16),...  101 us
    unnamed x9, local copies, waits for them, and re-layouts  5.84 us

profile of v1, /device:TPU:6, one launch (start us, length us, event | category | flops | bytes accessed | tf_op | source)
XLA Modules:
  0.0 111.2 jit_solution(1119502553647584604)
XLA Ops:
  0.6 0.8 slice.6
  1.4 0.7 slice.7
  2.1 0.9 stack.20.ids
  3.1 0.0 copy-start
  3.1 1.5 %copy-done = bf16[128,7168]{1,0:T(8,128)(2,1)S(1)} copy-done((bf16[128,7168]{1,0:T(8,128)(2,1)S(1)}, bf16[128,7168]{1,0:T(8,128)(2,1)}, u32[]{:S(2)}) %copy-start) | copy-done | bytes 1835032
  4.6 0.0 copy-start.1
  4.6 0.9 copy-done.1
  5.5 0.0 copy-start.2
  5.5 0.9 copy-done.2
  6.4 100.6 %shard_map.84 = (bf16[6,7168]{1,0:T(8,128)(2,1)S(1)}, bf16[128,7168]{1,0:T(8,128)(2,1)S(1)}, bf16[6,7168]{1,0:T(8,128)(2,1)S(1)}, f32[1,1]{1,0:T(1,128)}) custom-call(bf16[6,7168]{1,0:T(8,128)(2,1)S(1)} %copy-done.2, bf16[128,7168]{1,0:T(8,128)(2,1)S(1)} %copy-done, s32[8,192]{1,0:T(8,128)S(1)} %stack.20.ids, f32[192,192]{1,0:T(8,128)S(1)} %copy-done.1), custom_call_target="tpu_custom_call" | custom-call | tf_op jit(solution)/shard_map/pallas_call | solution.py:319
  107.0 0.6 copy.13
  107.6 1.2 %copy.14 = bf16[128,7168]{1,0:T(8,128)(2,1)} copy(bf16[128,7168]{1,0:T(8,128)(2,1)S(1)} %get-tuple-element.17) | data formatting | bytes 3670016
  108.9 0.6 copy.15
  (2 shorter events, 0.0 us)
Async XLA Ops:
  3.1 1.5 %copy-start = (bf16[128,7168]{1,0:T(8,128)(2,1)S(1)}, bf16[128,7168]{1,0:T(8,128)(2,1)}, u32[]{:S(2)}) copy-start(bf16[128,7168]{1,0:T(8,128)(2,1)} %w_ref.1) | copy-start | bytes 5505028
  4.6 0.9 copy-start.1
  5.5 0.9 copy-start.2

commit v2 on v1

v2 whole, which is shorter than its diff:
```python
import functools

import jax
import jax.numpy as jnp
from jax import lax
from jax.experimental import pallas as pl
from jax.experimental.pallas import tpu as pltpu
from jax.sharding import PartitionSpec as P

MESH = pl.DeviceIdType.MESH
LOSS_SCALE = 4096.0
TURNS = 16
TOKENS = 192
WIDTH = 7168
PIECE = 896
VROWS = 128
BF16 = jnp.bfloat16
F32 = jnp.float32


def kernel(
    hid, w_hbm, tok_in, seg_in,
    rowg, wgrad, trow, loss,
    hidv, w_ref, sbuf, scr48, hp, wg, acc, e_own, st, stx, sty, stz, eb, lgb, pf, pb, hb, r1, rh, hsum, h2s, h2,
    r2s, r2, gs, gb, rowf, wgs,
    lsem, ss0, ss1, sr, ws, wr, ys, yr, zus, zds, zr, cs, cr, xs, xr, es, er, tys, tyr, tzs, tzr,
    r1ss, r1rs, rhss, rhrs, h2ss, h2rs, r2ss, r2rs, gss, grs, outsem,
):
    pipe, dp = lax.axis_index("pipe"), lax.axis_index("dp")
    lo, y = pipe // 8, lax.rem(pipe, 8)
    h, j = dp // 8, lax.rem(dp, 8)
    x, c = j // 2, lax.rem(j, 2)
    z = h * 3 + lo

    def dev(jj, yy, zz):
        return (lax.rem(zz, 3) * 8 + yy, (zz // 3) * 8 + jj)

    sends = []

    def send(src, dst, ss, rs, to, cond=None):
        d = pltpu.make_async_remote_copy(
            src_ref=src, dst_ref=dst, send_sem=ss, recv_sem=rs, device_id=to, device_id_type=MESH
        )
        if cond is None:
            d.start()
        else:
            pl.when(cond)(d.start)
        sends.append((d, cond))

    def recv(dst, ss, rs, cond=None):
        d = pltpu.make_async_remote_copy(
            src_ref=dst, dst_ref=dst, send_sem=ss, recv_sem=rs,
            device_id=dev(j, lax.rem(y + 1, 8), z), device_id_type=MESH,
        )
        if cond is None:
            d.wait_recv()
        else:
            pl.when(cond)(d.wait_recv)

    loads = [
        pltpu.make_async_copy(a, b, lsem.at[i])
        for i, (a, b) in enumerate(((hid, hidv), (w_hbm, w_ref)))
    ]
    bar = pltpu.get_barrier_semaphore()

    def hello(to):
        pl.semaphore_signal(bar, inc=1, device_id=to, device_id_type=MESH)

    for dz in (6, 5, 7, 4, 8, 3, 9, 2, 10, 1, 11):
        hello(dev(j, y, lax.rem(z + dz, 12)))
    for dy in (4, 3, 5, 2, 6, 1, 7):
        hello(dev(j, lax.rem(y + dy, 8), z))
    for dj in range(1, 8):
        hello(dev(lax.rem(j + dj, 8), y, z))
    near_z = jnp.where(c == 0, lax.rem(z + 11, 12), lax.rem(z + 1, 12))
    for cc in range(2):
        hello(dev(x * 2 + cc, y, near_z))
    from_z = lax.rem(z + 3 + 3 * lo, 12)

    @pl.when(c == 1)
    def _():
        for jj in range(8):
            hello(dev(jj, y, from_z))

    for d in loads:
        d.start()

    pl.semaphore_wait(bar, 25 + 2 + 4)

    col = pl.ds(pl.multiple_of(y * PIECE, 128), PIECE)
    far_z = lax.rem(z + 9 - 3 * lo, 12)
    for dx in (2, 1, 3, 0):
        tx = lax.rem(x + dx, 4)
        send(hid.at[:, col], sbuf.at[j], ss1.at[dx], sr.at[j], dev(tx * 2 + 1, y, far_z))
    for dx in (2, 1, 3, 0):
        tx = lax.rem(x + dx, 4)
        send(
            hid.at[:, col], sbuf.at[j], ss0.at[dx], sr.at[j], dev(tx * 2, y, z),
            (c != 0) if dx == 0 else None,
        )

    def send_w(dj):
        tj = lax.rem(j + dj, 8)
        send(
            w_hbm.at[:, pl.ds(pl.multiple_of(tj * PIECE, 128), PIECE)], wg.at[j],
            ws.at[dj], wr.at[j], dev(tj, y, z),
        )

    def shifted(v, fill):
        return jnp.concatenate([v[:, 2:], jnp.full((1, 2), fill, jnp.int32)], axis=1)

    tok_ahead = shifted(tok_in[...], 0)
    seg = seg_in[...]
    seg_ahead = shifted(seg, -1)
    valid = (seg_ahead == seg).astype(F32)
    member = (lax.broadcasted_iota(jnp.int32, (TURNS, TOKENS), 0) == seg).astype(F32)
    counts = jnp.sum(member * valid, axis=1, keepdims=True)
    per_token = jnp.sum(member * counts, axis=0, keepdims=True)
    weight = valid / (jnp.maximum(per_token, 1.0) * TURNS)
    scaled = LOSS_SCALE * weight
    pick6 = (
        lax.broadcasted_iota(jnp.int32, (6, TOKENS), 1)
        == lax.broadcasted_iota(jnp.int32, (6, TOKENS), 0) + dp * 6
    )
    own_scaled = jnp.sum(jnp.where(pick6, scaled, 0.0), axis=1, keepdims=True)
    row = lax.broadcasted_iota(jnp.int32, (TOKENS, TOKENS), 0)
    six = lax.shift_right_logical(row * 10923, 16)
    token_of = (six & 3) * 48 + lax.shift_right_logical(six, 2) * 6 + (row - six * 6)
    perm = (lax.broadcasted_iota(jnp.int32, (TOKENS, TOKENS), 1) == token_of).astype(F32)

    def columns(rows, order=perm):
        return lax.dot_general(
            order, rows, (((1,), (1,)), ((), ())),
            preferred_element_type=F32, precision=lax.Precision.HIGHEST,
        )

    st[0:8, :] = jnp.broadcast_to(tok_ahead.astype(F32), (8, TOKENS))
    zed = lax.shift_right_logical(row, 4)
    third = lax.shift_right_logical(zed * 21846, 16)
    token_of = third * 48 + (lax.shift_right_logical(row, 1) & 7) * 6 + (zed - third * 3) * 2 + (row & 1)
    order = (lax.broadcasted_iota(jnp.int32, (TOKENS, TOKENS), 1) == token_of).astype(F32)
    ahead_col = jnp.round(columns(st[0:8, :], order)[:, 0:1]).astype(jnp.int32)
    loads[0].wait()
    trow[...] = (-own_scaled * hidv[...].astype(F32)).astype(BF16)

    loads[1].wait()
    wg[j] = w_ref[:, pl.ds(pl.multiple_of(j * PIECE, 128), PIECE)]

    @pl.when(c == 0)
    def _():
        sbuf[j] = hidv[:, col]

    for jj in range(8):
        recv(sbuf.at[jj], ss0.at[0], sr.at[jj], jnp.logical_or(jj != j, c == 1))
    for jj in range(8):
        scr48[6 * jj:6 * jj + 6, :] = sbuf[jj].astype(F32)
    ring_of = (h, lax.rem(h + 1 + lo, 4))
    zed_of = (
        lax.rem(h + jnp.where(lo == 0, 3, lo), 4),
        lax.rem(h + jnp.where(lo == 2, 1, lo + 2), 4),
    )

    def mine(pair):
        return jnp.where(c == 0, pair[0], pair[1])

    def other(pair):
        return jnp.where(c == 0, pair[1], pair[0])

    ring_b, zed_b, sib_ring, sib_zed = mine(ring_of), mine(zed_of), other(ring_of), other(zed_of)
    hp[y, ring_b] = scr48[...].astype(BF16)

    right, left = dev(j, lax.rem(y + 1, 8), z), dev(j, lax.rem(y + 7, 8), z)
    above, below = dev(x * 2, y, lax.rem(z + 1, 12)), dev(x * 2 + 1, y, lax.rem(z + 11, 12))
    sib = dev(x * 2 + 1 - c, y, z)
    sends_up = c == jnp.where(lo < 2, 1, 0)
    sends_down = c == jnp.where(lo > 0, 1, 0)

    def slot(k, way):
        return 0 if k == 0 else (7 if k == 4 else 1 + 2 * (k - 1) + way)

    def piece(k, way):
        return y if k == 0 else lax.rem(y + (8 - k if way == 0 else k), 8)

    def pass_on(k, way):
        n = slot(k, way)
        blk = hp.at[piece(k, way), ring_b]
        for w in (0, 1):
            if (k == 0 or w == way) and k < 4:
                send(
                    blk, blk, ys.at[w, k], yr.at[w, k], right if w == 0 else left,
                    (c == w) if k == 3 else None,
                )
        send(blk, blk, zus.at[n], zr.at[n], above, sends_up)
        send(blk, blk, zds.at[n], zr.at[n], below, sends_down)
        send(blk, blk, cs.at[n, 0], cr.at[n, 0], sib)

    def zed_on(k, way):
        n = slot(k, way)
        blk = hp.at[piece(k, way), zed_b]
        recv(blk, zus.at[n], zr.at[n])
        send(blk, blk, cs.at[n, 1], cr.at[n, 1], sib)

    def logits_of(k, way):
        n, p = slot(k, way), piece(k, way)
        recv(hp.at[p, sib_ring], cs.at[n, 0], cr.at[n, 0])
        recv(hp.at[p, sib_zed], cs.at[n, 1], cr.at[n, 1])
        tile = w_ref[:, pl.ds(pl.multiple_of(p * PIECE, 128), PIECE)]
        tokens = hp[p].reshape(TOKENS, PIECE)
        part = lax.dot_general(tile, tokens, (((1,), (1,)), ((), ())), preferred_element_type=F32)
        if k == 0:
            acc[...] = part
        else:
            acc[...] += part

    def ways(k):
        return (0,) if k in (0, 4) else (0, 1)

    pass_on(0, 0)
    for dj in W_FIRST:
        send_w(dj)
    for k in range(1, 5):
        if k == 4:
            recv(hp.at[piece(4, 0), ring_b], ys.at[c, 3], yr.at[c, 3])
            pass_on(4, 0)
        else:
            for way in (0, 1):
                recv(hp.at[piece(k, way), ring_b], ys.at[way, k - 1], yr.at[way, k - 1])
                pass_on(k, way)
        for dj in W_LATER[k - 1]:
            send_w(dj)
        for way in ways(k - 1):
            zed_on(k - 1, way)
        if k >= 2:
            for way in ways(k - 2):
                logits_of(k - 2, way)
    zed_on(4, 0)
    for way in ways(3):
        logits_of(3, way)
    logits_of(4, 0)

    logits = acc[...]
    vocab0 = (pipe * 32 + dp) * VROWS
    hit = lax.broadcasted_iota(jnp.int32, (VROWS, TOKENS), 0) == tok_ahead - vocab0
    peak = jnp.max(logits, axis=0, keepdims=True)
    ex = jnp.exp(logits - peak)
    e_own[...] = ex
    rest = jnp.where(hit, 0.0, ex)
    total = jnp.sum(rest, axis=0, keepdims=True)
    picked = jnp.sum(jnp.where(hit, logits, 0.0), axis=0, keepdims=True)

    def merge(buf, n):
        m = buf[0, 0:1, :]
        for i in range(1, n):
            m = jnp.maximum(m, buf[i, 0:1, :])
        s, p = jnp.zeros_like(m), jnp.zeros_like(m)
        for i in range(n):
            s += buf[i, 1:2, :] * jnp.exp(buf[i, 0:1, :] - m)
            p += buf[i, 2:3, :]
        return m, s, p

    def put(buf, idx, m, s, p):
        buf[idx, 0:1, :] = m
        buf[idx, 1:2, :] = s
        buf[idx, 2:3, :] = p
        buf[idx, 3:8, :] = jnp.zeros((5, TOKENS), F32)

    eb[j] = lax.dot_general(
        perm.astype(BF16), rest.astype(BF16), (((1,), (1,)), ((), ())), preferred_element_type=F32
    ).astype(BF16)
    put(stx, j, peak, total, picked)
    for dj in range(1, 8):
        send(stx.at[j], stx.at[j], xs.at[dj], xr.at[j], dev(lax.rem(j + dj, 8), y, z))
    for dj in range(1, 8):
        send(eb.at[j], eb.at[j], es.at[dj], er.at[j], dev(lax.rem(j + dj, 8), y, z))

    for jj in range(8):
        recv(wg.at[jj], ws.at[0], wr.at[jj], jj != j)
    lane = lax.broadcasted_iota(jnp.int32, (TOKENS, 8 * VROWS), 1)
    one = (lane == ahead_col - (pipe * 32 + h * 8) * VROWS).astype(F32).astype(BF16)
    w_all = wg[...].reshape(8 * VROWS, PIECE)
    hb[...] = jnp.dot(one, w_all, preferred_element_type=F32).astype(BF16).reshape(12, 16, PIECE)
    for dz in range(1, 12):
        tz = lax.rem(z + dz, 12)
        send(hb.at[tz], rh.at[z], rhss.at[dz], rhrs.at[z], dev(j, y, tz))

    for jj in range(8):
        recv(stx.at[jj], xs.at[0], xr.at[jj], jj != j)
    mx, sx, px = merge(stx, 8)
    put(sty, y, mx, sx, px)
    for dy in range(1, 8):
        send(sty.at[y], sty.at[y], tys.at[dy], tyr.at[y], dev(j, lax.rem(y + dy, 8), z))

    for jj in range(8):
        st[jj:jj + 1, :] = jnp.exp(stx[jj, 0:1, :] - mx)
    cols = columns(st[0:8, :])
    for jj in range(8):
        recv(eb.at[jj], es.at[0], er.at[jj], jj != j)
        lgb[:, jj * VROWS:(jj + 1) * VROWS] = (cols[:, jj:jj + 1] * eb[jj].astype(F32)).astype(BF16)
    part = jnp.dot(lgb[...], w_all, preferred_element_type=F32)
    pf[...] = part.reshape(8, 24, PIECE)
    pb[...] = pf[...].astype(BF16)
    for dy in range(1, 8):
        ty = lax.rem(y + dy, 8)
        send(pb.at[ty], r1.at[y], r1ss.at[dy], r1rs.at[y], dev(j, ty, z))

    for yy in range(8):
        recv(sty.at[yy], tys.at[0], tyr.at[yy], yy != y)
    my, sy, py = merge(sty, 8)
    put(stz, z, my, sy, py)
    for dz in range(1, 12):
        send(stz.at[z], stz.at[z], tzs.at[dz], tzr.at[z], dev(j, y, lax.rem(z + dz, 12)))
    for yy in range(8):
        st[yy:yy + 1, :] = jnp.exp(sty[yy, 0:1, :] - my)
    row24 = lax.broadcasted_iota(jnp.int32, (24, TOKENS), 0)
    six24 = lax.shift_right_logical(row24 * 10923, 16)
    pick24 = lax.broadcasted_iota(jnp.int32, (24, TOKENS), 1) == six24 * 48 + y * 6 + (row24 - six24 * 6)
    cols_y = columns(st[0:8, :], pick24.astype(F32))

    for zz in range(12):
        recv(stz.at[zz], tzs.at[0], tzr.at[zz], zz != z)
    m_all, s_rest, picked_all = merge(stz, 12)
    s_all = s_rest + jnp.exp(picked_all - m_all)
    log_total = m_all + jnp.log(s_all)
    loss[...] = jnp.sum(weight * (log_total - picked_all), axis=1, keepdims=True)
    for zz in range(12):
        st[zz:zz + 1, :] = scaled * jnp.exp(stz[zz, 0:1, :] - log_total)
    st[12:13, :] = (scaled * (s_rest / s_all)).astype(BF16).astype(F32)
    st[13:16, :] = jnp.zeros((3, TOKENS), F32)
    first = h * 48 + y * 6 + 2 * lo
    pick2 = (
        lax.broadcasted_iota(jnp.int32, (8, TOKENS), 1)
        == lax.broadcasted_iota(jnp.int32, (8, TOKENS), 0) + first
    )
    cols_z = columns(st[...], pick2.astype(F32))

    probs = (scaled * (e_own[...] * jnp.exp(peak - log_total))).astype(BF16)
    for p in range(8):
        wgs[:, p * PIECE:(p + 1) * PIECE] = jnp.dot(
            probs, hp[p].reshape(TOKENS, PIECE), preferred_element_type=F32
        ).astype(BF16)
    out = pltpu.make_async_copy(wgs, wgrad, outsem)
    out.start()

    rh[z] = hb[z]
    hsum[...] = jnp.zeros((16, PIECE), F32)
    for zz in range(12):
        recv(rh.at[zz], rhss.at[0], rhrs.at[zz], zz != z)
        hsum[...] += rh[zz].astype(F32)
    for yy in range(8):
        h2s[yy] = hsum[2 * yy:2 * yy + 2, :].astype(BF16)
    for dy in range(1, 8):
        ty = lax.rem(y + dy, 8)
        send(h2s.at[ty], h2.at[y], h2ss.at[dy], h2rs.at[y], dev(j, ty, z))

    r1[y] = jnp.zeros((24, PIECE), BF16)
    tot = pf[y] * jnp.sum(
        jnp.where(lax.broadcasted_iota(jnp.int32, (24, 8), 1) == y, cols_y, 0.0), axis=1, keepdims=True
    )
    for yy in range(8):
        recv(r1.at[yy], r1ss.at[0], r1rs.at[yy], yy != y)
        tot += cols_y[:, yy:yy + 1] * r1[yy].astype(F32)
    for zz in range(12):
        r2s[zz] = tot[2 * zz:2 * zz + 2, :].astype(BF16)
    for dz in range(1, 12):
        tz = lax.rem(z + dz, 12)
        send(r2s.at[tz], r2.at[z], r2ss.at[dz], r2rs.at[z], dev(j, y, tz))
    r2[z] = r2s[z]
    h2[y] = h2s[y]
    target = jnp.zeros((2, PIECE), F32)
    for yy in range(8):
        recv(h2.at[yy], h2ss.at[0], h2rs.at[yy], yy != y)
        target += h2[yy].astype(F32)
    fin = -cols_z[0:2, 12:13] * target
    for zz in range(12):
        recv(r2.at[zz], r2ss.at[0], r2rs.at[zz], zz != z)
        fin += cols_z[0:2, zz:zz + 1] * r2[zz].astype(F32)
    gs[...] = fin.astype(BF16)

    for l3 in range(3):
        for yy in range(8):
            to = dev(y, yy, h * 3 + l3)
            away = jnp.logical_or(jnp.logical_or(j != y, yy != y), lo != l3)
            send(gs, gb.at[lo, j], gss.at[l3, yy], grs.at[lo, j], to, away)

    @pl.when(j == y)
    def _():
        gb[lo, j] = gs[...]

    for l3 in range(3):
        for jj in range(8):
            away = jnp.logical_or(jnp.logical_or(j != y, jj != j), lo != l3)
            recv(gb.at[l3, jj], gss.at[0, 0], grs.at[l3, jj], away)
            rowf[2 * l3:2 * l3 + 2, jj * PIECE:(jj + 1) * PIECE] = gb[l3, jj].astype(F32)
    rowg[...] = rowf[0:6, :].astype(BF16)

    for d, cond in sends:
        if cond is None:
            d.wait_send()
        else:
            pl.when(cond)(d.wait_send)
    out.wait()


W_FIRST = (1, 2, 3, 4, 5, 6, 7)
W_LATER = ((), (), (), ())


def body(hidden, head_weight, token_ids, segment_ids):
    dma = pltpu.SemaphoreType.DMA
    vmem = pl.BlockSpec(memory_space=pltpu.VMEM)
    hbm = pl.BlockSpec(memory_space=pltpu.HBM)
    row_grad, weight_grad, target_rows, loss = pl.pallas_call(
        kernel,
        out_shape=(
            jax.ShapeDtypeStruct((6, WIDTH), BF16),
            jax.ShapeDtypeStruct((VROWS, WIDTH), BF16),
            jax.ShapeDtypeStruct((6, WIDTH), BF16),
            jax.ShapeDtypeStruct((1, 1), F32),
        ),
        in_specs=[hbm, hbm, vmem, vmem],
        out_specs=(vmem, hbm, vmem, vmem),
        scratch_shapes=[
            pltpu.VMEM((6, WIDTH), BF16),
            pltpu.VMEM((VROWS, WIDTH), BF16),
            pltpu.VMEM((8, 6, PIECE), BF16),
            pltpu.VMEM((48, PIECE), F32),
            pltpu.VMEM((8, 4, 48, PIECE), BF16),
            pltpu.VMEM((8, VROWS, PIECE), BF16),
            pltpu.VMEM((VROWS, TOKENS), F32),
            pltpu.VMEM((VROWS, TOKENS), F32),
            pltpu.VMEM((16, TOKENS), F32),
            pltpu.VMEM((8, 8, TOKENS), F32),
            pltpu.VMEM((8, 8, TOKENS), F32),
            pltpu.VMEM((12, 8, TOKENS), F32),
            pltpu.VMEM((8, TOKENS, VROWS), BF16),
            pltpu.VMEM((TOKENS, 8 * VROWS), BF16),
            pltpu.VMEM((8, 24, PIECE), F32),
            pltpu.VMEM((8, 24, PIECE), BF16),
            pltpu.VMEM((12, 16, PIECE), BF16),
            pltpu.VMEM((8, 24, PIECE), BF16),
            pltpu.VMEM((12, 16, PIECE), BF16),
            pltpu.VMEM((16, PIECE), F32),
            pltpu.VMEM((8, 2, PIECE), BF16),
            pltpu.VMEM((8, 2, PIECE), BF16),
            pltpu.VMEM((12, 2, PIECE), BF16),
            pltpu.VMEM((12, 2, PIECE), BF16),
            pltpu.VMEM((2, PIECE), BF16),
            pltpu.VMEM((3, 8, 2, PIECE), BF16),
            pltpu.VMEM((8, WIDTH), F32),
            pltpu.VMEM((VROWS, WIDTH), BF16),
            dma((2,)), dma((4,)), dma((4,)), dma((8,)), dma((8,)), dma((8,)),
            dma((2, 4)), dma((2, 4)), dma((8,)), dma((8,)), dma((8,)), dma((8, 2)), dma((8, 2)),
            dma((8,)), dma((8,)), dma((8,)), dma((8,)), dma((8,)), dma((8,)), dma((12,)), dma((12,)),
            dma((8,)), dma((8,)), dma((12,)), dma((12,)), dma((8,)), dma((8,)), dma((12,)), dma((12,)),
            dma((3, 8)), dma((3, 8)), dma,
        ],
        compiler_params=pltpu.CompilerParams(
            collective_id=0, has_side_effects=True, vmem_limit_bytes=56 * 2**20
        ),
    )(hidden, head_weight, token_ids.reshape(1, TOKENS), segment_ids.reshape(1, TOKENS))
    return (row_grad, weight_grad, target_rows, loss.reshape(()))


def solution(mesh):
    placed = (P("dp", None), P(("pipe", "dp"), None), P(), P())
    return jax.shard_map(
        body,
        mesh=mesh,
        in_specs=placed,
        out_specs=(P("dp", None), P(("pipe", "dp"), None), P("dp", None), P()),
        check_vma=False,
    )
```

time: 112 us -> 89.2 us (0.80)
  the two profiles are of different devices: /device:TPU:6 before, /device:TPU:4 now
where the time goes in v2:
time: 89.2 us; the launch traced here: 89 us
  Pallas kernels  81.5 us (91%)
  local copies, waits for them, and re-layouts  5.08 us (6%)
  between operations  2.39 us (3%)
    pallas_call x1, Pallas kernels, body(): pl.pallas_call(kernel, out_shape=(jax.ShapeDtypeStruct((6, WIDTH), BF16),...  81.5 us
    unnamed x5, local copies, waits for them, and re-layouts  5.08 us

profile of v2, /device:TPU:4, one launch (start us, length us, event | category | flops | bytes accessed | tf_op | source)
XLA Modules:
  0.0 89.0 jit_solution(9173773116525639060)
XLA Ops:
  0.6 81.5 %shard_map.75 = (bf16[6,7168]{1,0:T(8,128)(2,1)}, bf16[128,7168]{1,0:T(8,128)(2,1)}, bf16[6,7168]{1,0:T(8,128)(2,1)}, f32[1,1]{1,0:T(1,128)}) custom-call(bf16[6,7168]{1,0:T(8,128)(2,1)} %hid.1, bf16[128,7168]{1,0:T(8,128)(2,1)} %w_hbm.1, s32[1,192]{1,0:T(1,128)} %bitcast.3, s32[1,192]{1,0:T(1,128)} %bitcast.4), custom_call_target="tpu_custom_call" | custom-call | tf_op jit(solution)/shard_map/pallas_call | solution.py:412
  82.1 1.6 %copy.12 = bf16[6,7168]{1,0:T(8,128)(2,1)} copy(bf16[6,7168]{1,0:T(8,128)(2,1)} %get-tuple-element.16) | data formatting | bytes 172032
  83.7 0.0 copy-start
  83.7 2.9 %copy.13 = bf16[128,7168]{1,0:T(8,128)(2,1)} copy(bf16[128,7168]{1,0:T(8,128)(2,1)} %get-tuple-element.17) | data formatting | bytes 3670016
  86.6 0.0 copy-done
  86.6 0.6 copy.14
Async XLA Ops:
  83.7 2.9 %copy-start = (bf16[6,7168]{1,0:T(8,128)(2,1)S(1)}, bf16[6,7168]{1,0:T(8,128)(2,1)}, u32[]{:S(2)}) copy-start(bf16[6,7168]{1,0:T(8,128)(2,1)} %get-tuple-element.18) | copy-start | bytes 258052

commit v3 on v2

--- a/solution.py
+++ b/solution.py
@@ -46,6 +46,14 @@
         else:
             pl.when(cond)(d.start)
         sends.append((d, cond))
+
+    def flush(keep=0):
+        while len(sends) > keep:
+            d, cond = sends.pop(0)
+            if cond is None:
+                d.wait_send()
+            else:
+                pl.when(cond)(d.wait_send)
 
     def recv(dst, ss, rs, cond=None):
         d = pltpu.make_async_remote_copy(
@@ -181,15 +189,21 @@
     def piece(k, way):
         return y if k == 0 else lax.rem(y + (8 - k if way == 0 else k), 8)
 
+    def part_of(k, way, sub):
+        return hp.at[piece(k, way), ring_b, :, pl.ds(*SUBS[sub])]
+
+    def ring_on(k, way, sub):
+        blk = part_of(k, way, sub)
+        for w in (0, 1):
+            if (k == 0 or w == way) and k < 4:
+                send(
+                    blk, blk, ys.at[w, k, sub], yr.at[w, k, sub], right if w == 0 else left,
+                    (c == w) if k == 3 else None,
+                )
+
     def pass_on(k, way):
         n = slot(k, way)
         blk = hp.at[piece(k, way), ring_b]
-        for w in (0, 1):
-            if (k == 0 or w == way) and k < 4:
-                send(
-                    blk, blk, ys.at[w, k], yr.at[w, k], right if w == 0 else left,
-                    (c == w) if k == 3 else None,
-                )
         send(blk, blk, zus.at[n], zr.at[n], above, sends_up)
         send(blk, blk, zds.at[n], zr.at[n], below, sends_down)
         send(blk, blk, cs.at[n, 0], cr.at[n, 0], sib)
@@ -215,16 +229,22 @@
     def ways(k):
         return (0,) if k in (0, 4) else (0, 1)
 
+    for sub in (0, 1):
+        ring_on(0, 0, sub)
     pass_on(0, 0)
     for dj in W_FIRST:
         send_w(dj)
     for k in range(1, 5):
         if k == 4:
-            recv(hp.at[piece(4, 0), ring_b], ys.at[c, 3], yr.at[c, 3])
+            for sub in (0, 1):
+                recv(part_of(4, 0, sub), ys.at[c, 3, sub], yr.at[c, 3, sub])
             pass_on(4, 0)
         else:
+            for sub in (0, 1):
+                for way in (0, 1):
+                    recv(part_of(k, way, sub), ys.at[way, k - 1, sub], yr.at[way, k - 1, sub])
+                    ring_on(k, way, sub)
             for way in (0, 1):
-                recv(hp.at[piece(k, way), ring_b], ys.at[way, k - 1], yr.at[way, k - 1])
                 pass_on(k, way)
         for dj in W_LATER[k - 1]:
             send_w(dj)
@@ -316,6 +336,29 @@
     pick24 = lax.broadcasted_iota(jnp.int32, (24, TOKENS), 1) == six24 * 48 + y * 6 + (row24 - six24 * 6)
     cols_y = columns(st[0:8, :], pick24.astype(F32))
 
+    rh[z] = hb[z]
+    hsum[...] = jnp.zeros((16, PIECE), F32)
+    for zz in range(12):
+        recv(rh.at[zz], rhss.at[0], rhrs.at[zz], zz != z)
+        hsum[...] += rh[zz].astype(F32)
+    for yy in range(8):
+        h2s[yy] = hsum[2 * yy:2 * yy + 2, :].astype(BF16)
+    for dy in range(1, 8):
+        ty = lax.rem(y + dy, 8)
+        send(h2s.at[ty], h2.at[y], h2ss.at[dy], h2rs.at[y], dev(j, ty, z))
+
+    r1[y] = jnp.zeros((24, PIECE), BF16)
+    tot = pf[y] * jnp.sum(
+        jnp.where(lax.broadcasted_iota(jnp.int32, (24, 8), 1) == y, cols_y, 0.0), axis=1, keepdims=True
+    )
+    for yy in range(8):
+        recv(r1.at[yy], r1ss.at[0], r1rs.at[yy], yy != y)
+        tot += cols_y[:, yy:yy + 1] * r1[yy].astype(F32)
+    for zz in range(12):
+        r2s[zz] = tot[2 * zz:2 * zz + 2, :].astype(BF16)
+    for dz in range(1, 12):
+        tz = lax.rem(z + dz, 12)
+        send(r2s.at[tz], r2.at[z], r2ss.at[dz], r2rs.at[z], dev(j, y, tz))
     for zz in range(12):
         recv(stz.at[zz], tzs.at[0], tzr.at[zz], zz != z)
     m_all, s_rest, picked_all = merge(stz, 12)
@@ -334,36 +377,17 @@
     cols_z = columns(st[...], pick2.astype(F32))
 
     probs = (scaled * (e_own[...] * jnp.exp(peak - log_total))).astype(BF16)
-    for p in range(8):
-        wgs[:, p * PIECE:(p + 1) * PIECE] = jnp.dot(
+
+    def one_piece(p, carry):
+        wgs[:, pl.ds(pl.multiple_of(p * PIECE, 128), PIECE)] = jnp.dot(
             probs, hp[p].reshape(TOKENS, PIECE), preferred_element_type=F32
         ).astype(BF16)
+        return carry
+
+    lax.fori_loop(0, 8, one_piece, 0)
     out = pltpu.make_async_copy(wgs, wgrad, outsem)
     out.start()
 
-    rh[z] = hb[z]
-    hsum[...] = jnp.zeros((16, PIECE), F32)
-    for zz in range(12):
-        recv(rh.at[zz], rhss.at[0], rhrs.at[zz], zz != z)
-        hsum[...] += rh[zz].astype(F32)
-    for yy in range(8):
-        h2s[yy] = hsum[2 * yy:2 * yy + 2, :].astype(BF16)
-    for dy in range(1, 8):
-        ty = lax.rem(y + dy, 8)
-        send(h2s.at[ty], h2.at[y], h2ss.at[dy], h2rs.at[y], dev(j, ty, z))
-
-    r1[y] = jnp.zeros((24, PIECE), BF16)
-    tot = pf[y] * jnp.sum(
-        jnp.where(lax.broadcasted_iota(jnp.int32, (24, 8), 1) == y, cols_y, 0.0), axis=1, keepdims=True
-    )
-    for yy in range(8):
-        recv(r1.at[yy], r1ss.at[0], r1rs.at[yy], yy != y)
-        tot += cols_y[:, yy:yy + 1] * r1[yy].astype(F32)
-    for zz in range(12):
-        r2s[zz] = tot[2 * zz:2 * zz + 2, :].astype(BF16)
-    for dz in range(1, 12):
-        tz = lax.rem(z + dz, 12)
-        send(r2s.at[tz], r2.at[z], r2ss.at[dz], r2rs.at[z], dev(j, y, tz))
     r2[z] = r2s[z]
     h2[y] = h2s[y]
     target = jnp.zeros((2, PIECE), F32)
@@ -386,6 +410,7 @@
     def _():
         gb[lo, j] = gs[...]
 
+    flush(24)
     for l3 in range(3):
         for jj in range(8):
             away = jnp.logical_or(jnp.logical_or(j != y, jj != j), lo != l3)
@@ -393,14 +418,11 @@
             rowf[2 * l3:2 * l3 + 2, jj * PIECE:(jj + 1) * PIECE] = gb[l3, jj].astype(F32)
     rowg[...] = rowf[0:6, :].astype(BF16)
 
-    for d, cond in sends:
-        if cond is None:
-            d.wait_send()
-        else:
-            pl.when(cond)(d.wait_send)
+    flush()
     out.wait()
 
 
+SUBS = ((0, 512), (512, 384))
 W_FIRST = (1, 2, 3, 4, 5, 6, 7)
 W_LATER = ((), (), (), ())
 
@@ -449,7 +471,7 @@
             pltpu.VMEM((8, WIDTH), F32),
             pltpu.VMEM((VROWS, WIDTH), BF16),
             dma((2,)), dma((4,)), dma((4,)), dma((8,)), dma((8,)), dma((8,)),
-            dma((2, 4)), dma((2, 4)), dma((8,)), dma((8,)), dma((8,)), dma((8, 2)), dma((8, 2)),
+            dma((2, 4, 2)), dma((2, 4, 2)), dma((8,)), dma((8,)), dma((8,)), dma((8, 2)), dma((8, 2)),
             dma((8,)), dma((8,)), dma((8,)), dma((8,)), dma((8,)), dma((8,)), dma((12,)), dma((12,)),
             dma((8,)), dma((8,)), dma((12,)), dma((12,)), dma((8,)), dma((8,)), dma((12,)), dma((12,)),
             dma((3, 8)), dma((3, 8)), dma,

time: 89.2 us -> 87.9 us (0.985)
  Pallas kernels: 81.5 us -> 80.2 us
    pallas_call x1, Pallas kernels: 81.5 us -> 80.2 us  [body(): pl.pallas_call(kernel, out_shape=(jax.ShapeDtypeStruct((6, WIDTH), BF16),...]
where the time goes in v3:
time: 87.9 us; the launch traced here: 87.7 us
  Pallas kernels  80.2 us (91%)
  local copies, waits for them, and re-layouts  5.08 us (6%)
  between operations  2.39 us (3%)
    pallas_call x1, Pallas kernels, body(): pl.pallas_call(kernel, out_shape=(jax.ShapeDtypeStruct((6, WIDTH), BF16),...  80.2 us
    unnamed x5, local copies, waits for them, and re-layouts  5.08 us

profile of v3, /device:TPU:4, one launch (start us, length us, event | category | flops | bytes accessed | tf_op | source)
XLA Modules:
  0.0 87.7 jit_solution(460697679189401918)
XLA Ops:
  0.6 80.2 %shard_map.75 = (bf16[6,7168]{1,0:T(8,128)(2,1)}, bf16[128,7168]{1,0:T(8,128)(2,1)}, bf16[6,7168]{1,0:T(8,128)(2,1)}, f32[1,1]{1,0:T(1,128)}) custom-call(bf16[6,7168]{1,0:T(8,128)(2,1)} %hid.1, bf16[128,7168]{1,0:T(8,128)(2,1)} %w_hbm.1, s32[1,192]{1,0:T(1,128)} %bitcast.3, s32[1,192]{1,0:T(1,128)} %bitcast.4), custom_call_target="tpu_custom_call" | custom-call | tf_op jit(solution)/shard_map/pallas_call | solution.py:434
  80.9 1.6 %copy.12 = bf16[6,7168]{1,0:T(8,128)(2,1)} copy(bf16[6,7168]{1,0:T(8,128)(2,1)} %get-tuple-element.16) | data formatting | bytes 172032
  82.4 0.0 copy-start
  82.4 2.9 %copy.13 = bf16[128,7168]{1,0:T(8,128)(2,1)} copy(bf16[128,7168]{1,0:T(8,128)(2,1)} %get-tuple-element.17) | data formatting | bytes 3670016
  85.3 0.0 copy-done
  85.3 0.6 copy.14
Async XLA Ops:
  82.4 2.9 %copy-start = (bf16[6,7168]{1,0:T(8,128)(2,1)S(1)}, bf16[6,7168]{1,0:T(8,128)(2,1)}, u32[]{:S(2)}) copy-start(bf16[6,7168]{1,0:T(8,128)(2,1)} %get-tuple-element.18) | copy-start | bytes 258052
